TPU v7x, 32 devices: a whole 2x2x4 slice. The times are simulated.
32 devices in a mesh: feat: 8 (over y, x, core), node: 4 (over z).
Axes of the slice: x: 2, y: 2, z: 4, core: 2. Of those that a mesh axis runs over, the one named last changes fastest.
Arguments:
- features: bfloat16 [4, 512, 16384], P('node', 'feat'), may hold values from -6 to 6
- target_ids: int32 [4, 4096], P('node'), may hold values from 0 to 16383
- block_ids: int32 [4, 32, 8], P('node'), may hold values from 0 to 127
- tile_counts: int32 [4, 32], P('node'), may hold values from 1 to 8, as said below
- adjacency: bfloat16 [4, 32, 8, 128, 128], P('node'), may hold values from 0 to 0.25
- w_neigh: bfloat16 [256, 512], P(None, 'feat'), may hold values from -0.1875 to 0.1875
- w_self: bfloat16 [256, 512], P(None, 'feat'), may hold values from -0.1875 to 0.1875
- w_head: bfloat16 [256, 256], replicated, may hold values from -0.375 to 0.375
- grad_scores: bfloat16 [4, 4096, 256], P('node', 'feat'), may hold values from -6 to 6
Outputs:
- scores: bfloat16 [4, 4096, 256], P('node', 'feat')
- grad_head: float32 [256, 256], replicated
- grad_neigh: float32 [256, 512], P(None, 'feat')
- grad_self: float32 [256, 512], P(None, 'feat')
Inputs may be any that keep to these rules, and one draw needn't show every extreme that they name: `tile_counts`: one group, drawn from the seed, has all of its tiles at 8 live slots; every tile of the other groups has fewer than 8.
All inputs are finite; a program needn't handle non-finite values.
Results may differ from a plain program's by a relative error of at most 0.0056.
Values may be sent and summed in bfloat16 or wider, within the bound.
A program may use at most 64 MiB of HBM per device.

v0:
```python
import jax
import jax.numpy as jnp
from jax import lax
from jax.sharding import PartitionSpec as P


def aggregate_local(feature_rows, block_row, count_row, adjacency_group):
    width = feature_rows.shape[0]
    tiles = block_row.shape[0]
    slots = block_row.shape[1]
    blocks = feature_rows.reshape(width, -1, 128)
    gathered = jnp.take(blocks, block_row.reshape(-1), axis=1).reshape(width, tiles, slots, 128)
    live = (jnp.arange(slots, dtype=jnp.int32)[None, :] < count_row[:, None]).astype(jnp.bfloat16)
    masked = gathered * live[None, :, :, None]
    summed = jnp.einsum(
        "tkrs,ftks->ftr", adjacency_group, masked, preferred_element_type=jnp.float32
    )
    summed = summed / count_row.astype(jnp.float32)[None, :, None]
    return summed.astype(jnp.bfloat16).reshape(width, tiles * 128)


def contract_first(left, right):
    return lax.dot_general(
        left, right, (((0,), (1,)), ((), ())), preferred_element_type=jnp.float32
    )


def body(
    features, target_ids, block_ids, tile_counts, adjacency, w_neigh, w_self, w_head, grad_scores
):
    feature_rows = features[0]
    aggregate = aggregate_local(feature_rows, block_ids[0], tile_counts[0], adjacency[0])
    own = jnp.take(feature_rows, target_ids[0], axis=1)
    agg_part = aggregate
    own_part = own
    preact = lax.psum_scatter(
        contract_first(agg_part, w_neigh) + contract_first(own_part, w_self),
        "feat",
        scatter_dimension=0,
        tiled=True,
    )
    hidden = jax.nn.silu(preact).astype(jnp.bfloat16)
    scores = jnp.dot(hidden, w_head.T, preferred_element_type=jnp.float32).astype(jnp.bfloat16)
    cotangent = grad_scores[0]
    head_local = lax.dot_general(
        cotangent, hidden, (((0,), (0,)), ((), ())), preferred_element_type=jnp.float32
    )
    grad_head = lax.psum(head_local, ("feat", "node"))
    grad_hidden = jnp.dot(cotangent, w_head, preferred_element_type=jnp.float32)
    sigma = jax.nn.sigmoid(preact)
    grad_pre = (grad_hidden * sigma * (1.0 + preact * (1.0 - sigma))).astype(jnp.bfloat16)
    shard_piece = lax.all_gather(grad_pre, "feat", axis=0, tiled=True)
    agg_part = aggregate
    own_part = own
    neigh_local = contract_first(shard_piece, agg_part)
    self_local = contract_first(shard_piece, own_part)
    grad_neigh, grad_self = lax.psum((neigh_local, self_local), "node")
    return (scores[None], grad_head, grad_neigh, grad_self)


def solution(mesh):
    in_specs = (
        P("node", "feat", None),
        P("node", None),
        P("node", None, None),
        P("node", None),
        P("node", None, None, None, None),
        P(None, "feat"),
        P(None, "feat"),
        P(),
        P("node", "feat", None),
    )
    out_specs = (P("node", "feat", None), P(), P(None, "feat"), P(None, "feat"))
    return jax.shard_map(body, mesh=mesh, in_specs=in_specs, out_specs=out_specs, check_vma=False)
```

profile of v0, /device:TPU:0, one launch (start us, length us, event | category | flops | bytes accessed | tf_op | source)
XLA Modules:
  0.0 308.8 jit_solution(13335983999297234126)
XLA Ops:
  7.2 0.0 copy-start
  7.2 0.0 copy-start.1
  7.2 0.0 reduce-scatter.2.cloned.1.call-start
  7.2 0.8 compare_and_fusion.1
  8.1 0.8 copy.23
  8.8 0.7 bitcast_convert_fusion
  9.5 0.1 copy.22
  9.6 0.7 compare_select_fusion
  10.3 0.7 compare_and_fusion
  11.1 0.7 fusion.33
  11.8 0.1 reshape_squeeze.10
  11.9 4.8 %copy.26 = bf16[1,64,16384]{1,2,0:T(8,128)(2,1)} copy(bf16[1,64,16384]{2,1,0:T(8,128)(2,1)} %param.9) | data formatting | bytes 4194304 | tf_op args[0]
  16.7 0.0 copy-done.1
  16.7 0.6 copy.30
  17.3 1.4 copy.24
  18.6 3.1 gather_fusion
  21.7 13.8 %gather_fusion.1 = bf16[4096,64]{1,0:T(8,128)(2,1)S(1)} fusion(bf16[64,16384]{0,1:T(8,128)(2,1)} %bitcast.57, s32[4096]{0:T(1024)S(1)} %broadcast_clamp_fusion), kind=kCustom, calls=%fused_computation.1 | custom fusion | bytes 1064960 | tf_op jit(solution)/shard_map/jit(_take)/gather | solution.py:33
  35.5 0.0 copy-done.4
  35.5 0.0 copy-start.2
  35.5 1.5 fusion.29
  37.0 0.7 copy-done.2
  37.7 0.0 copy-start.5
  37.7 5.7 %fusion.19 = bf16[32,8,8,128]{3,2,1,0:T(8,128)(2,1)S(1)} fusion(bf16[1,32,8,128,128]{4,3,2,1,0:T(8,128)(2,1)} %param.13, bf16[64,32,8,128]{3,0,2,1:T(8,128)(2,1)S(1)} %bitcast.60, pred[32,8]{1,0:T(8,128)(4,1)S(1)} %copy.22, bf16[32,8]{1,0:T(8,128)(2,1)S(1)} %fusion.33, f32[32]{0:T(128)S(1)} %bitcast_convert_fusion), kind=kOutput, calls=%fused_computation.19 | convolution fusion | flops 541589504 | bytes 13108096 | tf_op jit(solution)/shard_map/tkrs,ftks->ftr/dot_general | solution.py:15
  43.4 0.0 copy-done.5
  43.4 2.7 convolution_add_fusion
  46.1 0.0 reduce-scatter.2.cloned.1.call-update
  46.1 0.0 all-gather.2.cloned.1.call-start
  46.2 54.1 %reduce-scatter.2.cloned.1.call-done = f32[512,256]{1,0:T(8,128)} async-done(((f32[4096,256]{1,0:T(8,128)}), f32[512,256]{1,0:T(8,128)}) %reduce-scatter.2.cloned.1.call-update) | async-done | bytes 524304 | tf_op jit(solution)/shard_map/reduce_scatter | solution.py:36
  100.3 0.0 copy-done
  100.3 0.0 copy-done.7
  100.3 2.0 fusion.13
  102.3 0.0 all-gather.2.cloned.1.call-update
  102.4 0.0 all-reduce.4.cloned.1.call-start
  102.4 2.1 convolution_bitcast_fusion
  104.5 0.0 all-reduce.4.cloned.1.call-update
  104.5 0.0 all-reduce.6.cloned.1.call-start
  104.6 26.3 %all-gather.2.cloned.1.call-done = bf16[4096,256]{1,0:T(8,128)(2,1)} async-done(((bf16[512,256]{1,0:T(8,128)(2,1)}), bf16[4096,256]{1,0:T(8,128)(2,1)}) %all-gather.2.cloned.1.call-update) | async-done | bytes 2097168 | tf_op jit(solution)/shard_map/all_gather | solution.py:52
  130.9 4.9 %fusion.30 = f32[256,64]{0,1:T(8,128)} fusion(bf16[4096,256]{1,0:T(8,128)(2,1)} %all-gather.2.cloned.1.call-done, bf16[4096,64]{1,0:T(8,128)(2,1)S(1)} %gather_fusion.1, pred[4096]{0:T(1024)(128)(4,1)S(1)} %compare_and_fusion), kind=kOutput, calls=%fused_computation.28 | convolution fusion | flops 134479872 | bytes 2691072 | tf_op jit(solution)/shard_map/dot_general | solution.py:23
  135.8 0.0 copy-done.3
  135.8 1.1 fusion.24
  136.9 0.0 all-reduce.6.cloned.1.call-update
  136.9 0.0 copy-done.6
  136.9 1.0 fusion.14
  137.9 124.9 %all-reduce.4.cloned.1.call-done = f32[256,256]{0,1:T(8,128)} async-done(((f32[256,256]{0,1:T(8,128)}), f32[256,256]{0,1:T(8,128)}) %all-reduce.4.cloned.1.call-update) | async-done | bytes 262160 | tf_op jit(solution)/shard_map/psum | solution.py:48
  262.9 1.8 copy.27
  264.6 34.7 %all-reduce.6.cloned.1.call-done = (f32[256,64]{0,1:T(8,128)}, f32[256,64]{0,1:T(8,128)}) async-done(((f32[256,64]{0,1:T(8,128)}, f32[256,64]{0,1:T(8,128)}), (f32[256,64]{0,1:T(8,128)}, f32[256,64]{0,1:T(8,128)})) %all-reduce.6.cloned.1.call-update) | async-done | bytes 131088 | tf_op jit(solution)/shard_map/psum | solution.py:57
  299.4 1.5 copy.42
  300.8 1.5 copy.43
  (7 shorter events, 0.0 us)
Async XLA Ops:
  7.2 93.1 %copy-start = (bf16[1,512,256]{2,1,0:T(8,128)(2,1)S(1)}, bf16[1,512,256]{2,1,0:T(8,128)(2,1)}, u32[]{:S(2)}) copy-start(bf16[1,512,256]{2,1,0:T(8,128)(2,1)} %param.17) | copy-start | bytes 786436
  7.2 9.5 %copy-start.1 = (bf16[1,64,16384]{2,1,0:T(8,128)(2,1)S(1)}, bf16[1,64,16384]{2,1,0:T(8,128)(2,1)}, u32[]{:S(2)}) copy-start(bf16[1,64,16384]{2,1,0:T(8,128)(2,1)} %param.9) | copy-start | bytes 6291460
  7.2 93.1 %reduce-scatter.2.cloned.1.call-start = ((), (), s32[]{:S(2)}) async-start(), calls=%async_computation.1 | async-start | bytes 4718592 | tf_op jit(solution)/shard_map/reduce_scatter | solution.py:36
  21.7 13.8 %copy-start.4 = (bf16[256,64]{0,1:T(8,128)(2,1)S(1)}, bf16[256,64]{0,1:T(8,128)(2,1)}, u32[]{:S(2)}) copy-start(bf16[256,64]{0,1:T(8,128)(2,1)} %param.15) | copy-start | bytes 98308
  35.5 2.2 copy-start.2
  37.7 5.7 %copy-start.5 = (bf16[256,64]{0,1:T(8,128)(2,1)S(1)}, bf16[256,64]{0,1:T(8,128)(2,1)}, u32[]{:S(2)}) copy-start(bf16[256,64]{0,1:T(8,128)(2,1)} %param.14) | copy-start | bytes 98308
  46.1 54.2 %copy-start.7 = (bf16[256,256]{1,0:T(8,128)(2,1)S(1)}, bf16[256,256]{1,0:T(8,128)(2,1)}, u32[]{:S(2)}) copy-start(bf16[256,256]{1,0:T(8,128)(2,1)} %param.16) | copy-start | bytes 393220
  46.1 84.7 %all-gather.2.cloned.1.call-start = ((), (), s32[]{:S(2)}) async-start(), calls=%async_computation.3 | async-start | bytes 2359296 | tf_op jit(solution)/shard_map/all_gather | solution.py:52
  102.4 160.5 %all-reduce.4.cloned.1.call-start = ((), (), s32[]{:S(2)}) async-start(), calls=%async_computation.2 | async-start | bytes 524288 | tf_op jit(solution)/shard_map/psum | solution.py:48
  104.5 32.5 %copy-start.6 = (f32[512,256]{1,0:T(8,128)S(1)}, f32[512,256]{1,0:T(8,128)}, u32[]{:S(2)}) copy-start(f32[512,256]{1,0:T(8,128)} %reduce-scatter.2.cloned.1.call-done) | copy-start | bytes 1572868
  104.5 194.9 %all-reduce.6.cloned.1.call-start = ((), (), s32[]{:S(2)}) async-start(), calls=%async_computation.4 | async-start | bytes 262144 | tf_op jit(solution)/shard_map/psum | solution.py:57
  130.8 4.9 %copy-start.3 = (bf16[4096,256]{1,0:T(8,128)(2,1)S(1)}, bf16[4096,256]{1,0:T(8,128)(2,1)}, u32[]{:S(2)}) copy-start(bf16[4096,256]{1,0:T(8,128)(2,1)} %all-gather.2.cloned.1.call-done) | copy-start | bytes 6291460
Sparse Core Ops, SparseCore 0:
  46.2 53.9 reduce-scatter.1
  102.9 27.8 all-gather.1
  137.8 124.9 all-reduce.3
  265.8 33.5 all-reduce.5
where the time goes:
time: 309 us
  waiting for transfers between devices  240 us (78%)
  local copies, waits for them, and re-layouts  30 us (10%)
  matrix products  21 us (7%)
  between operations  13.9 us (4%)
  other arithmetic  3.71 us (1%)
    psum x1, waiting for transfers between devices, body(): grad_head = lax.psum(head_local, ('feat', 'node'))  125 us
    reduce_scatter x1, waiting for transfers between devices, body(): lax.psum_scatter(contract_first(agg_part, w_neigh) + contract_first(own_p...  54.1 us
    psum x1, waiting for transfers between devices, body(): grad_neigh, grad_self = lax.psum((neigh_local, self_local), 'node')  34.7 us
    all_gather x1, waiting for transfers between devices, body(): shard_piece = lax.all_gather(grad_pre, 'feat', axis=0, tiled=True)  26.3 us
    gather x1, local copies, waits for them, and re-layouts, body(): own = jnp.take(feature_rows, target_ids[0], axis=1)  13.8 us
    unnamed x22, local copies, waits for them, and re-layouts  11.6 us
    dot_general x4, matrix products, contract_first(): lax.dot_general(left, right, (((0,), (1,)), ((), ())), preferred_element_...  10.2 us
  transfers between devices with their start and end apart: 4, of which 4 were waited for; matrix products, arithmetic and copies ran while one was open for 4% of the time, Pallas kernels for 0%

commit v1 on v0

--- a/solution.py
+++ b/solution.py
@@ -1,7 +1,17 @@
+import functools
 import jax
 import jax.numpy as jnp
 from jax import lax
 from jax.sharding import PartitionSpec as P
+
+
+def plan_quotas_in(incoming_x, mesh_name, net_axis):
+    step_out = jax.lax.psum(incoming_x, mesh_name)
+    val = jax.lax.psum(step_out, net_axis)
+    return val
+
+
+proceed_the_circles = functools.partial(plan_quotas_in, mesh_name="node", net_axis="feat")
 
 
 def aggregate_local(feature_rows, block_row, count_row, adjacency_group):
@@ -45,7 +55,7 @@
     head_local = lax.dot_general(
         cotangent, hidden, (((0,), (0,)), ((), ())), preferred_element_type=jnp.float32
     )
-    grad_head = lax.psum(head_local, ("feat", "node"))
+    grad_head = proceed_the_circles(head_local)
     grad_hidden = jnp.dot(cotangent, w_head, preferred_element_type=jnp.float32)
     sigma = jax.nn.sigmoid(preact)
     grad_pre = (grad_hidden * sigma * (1.0 + preact * (1.0 - sigma))).astype(jnp.bfloat16)

time: 309 us -> 242 us (0.78)
  waiting for transfers between devices: 240 us -> 173 us
    psum x2, waiting for transfers between devices: 160 us -> 92.2 us  [the longest x1 54.9 us: plan_quotas_in(): val = jax.lax.psum(step_out, net_axis)]
  transfers between devices with their start and end apart: 4 -> 4, of which waited for: 4 -> 4; matrix products, arithmetic and copies ran while one was open for 4% -> 1% of each run, Pallas kernels for 0% -> 0%
where the time goes in v1:
time: 242 us; the launch traced here: 241 us
  waiting for transfers between devices  173 us (71%)
  local copies, waits for them, and re-layouts  30 us (12%)
  matrix products  21 us (9%)
  between operations  13.9 us (6%)
  other arithmetic  3.71 us (2%)
    psum x1, waiting for transfers between devices, plan_quotas_in(): val = jax.lax.psum(step_out, net_axis)  54.9 us
    reduce_scatter x1, waiting for transfers between devices, body(): lax.psum_scatter(contract_first(agg_part, w_neigh) + contract_first(own_p...  54.1 us
    psum x1, waiting for transfers between devices, plan_quotas_in(): step_out = jax.lax.psum(incoming_x, mesh_name)  37.4 us
    all_gather x1, waiting for transfers between devices, body(): shard_piece = lax.all_gather(grad_pre, 'feat', axis=0, tiled=True)  26.4 us
    gather x1, local copies, waits for them, and re-layouts, body(): own = jnp.take(feature_rows, target_ids[0], axis=1)  13.8 us
    unnamed x22, local copies, waits for them, and re-layouts  11.6 us
    dot_general x4, matrix products, contract_first(): lax.dot_general(left, right, (((0,), (1,)), ((), ())), preferred_element_...  10.2 us
    dot_general x1, matrix products, aggregate_local(): jnp.einsum('tkrs,ftks->ftr', adjacency_group, masked, preferred_element_t...  5.64 us
  transfers between devices with their start and end apart: 4, of which 4 were waited for; matrix products, arithmetic and copies ran while one was open for 1% of the time, Pallas kernels for 0%

profile of v1, /device:TPU:0, one launch (start us, length us, event | category | flops | bytes accessed | tf_op | source)
XLA Modules:
  0.0 241.5 jit_solution(7593313731821987894)
XLA Ops:
  7.2 0.0 copy-start
  7.2 0.0 copy-start.1
  7.2 0.0 reduce-scatter.2.cloned.1.call-start
  7.2 0.8 compare_and_fusion.1
  8.1 0.8 copy.23
  8.8 0.7 bitcast_convert_fusion
  9.5 0.1 copy.22
  9.6 0.7 compare_select_fusion
  10.3 0.7 compare_and_fusion
  11.1 0.7 fusion.33
  11.8 0.1 reshape_squeeze.10
  11.9 4.8 %copy.26 = bf16[1,64,16384]{1,2,0:T(8,128)(2,1)} copy(bf16[1,64,16384]{2,1,0:T(8,128)(2,1)} %param.9) | data formatting | bytes 4194304 | tf_op args[0]
  16.7 0.0 copy-done.1
  16.7 0.6 copy.30
  17.3 1.4 copy.24
  18.6 3.1 %gather_fusion = bf16[256,64,128]{2,1,0:T(8,128)(2,1)} fusion(bf16[64,128,128]{2,0,1:T(8,128)(2,1)S(1)} %copy.24, s32[1024]{0:T(1024)S(1)} %pad_clamp_fusion), kind=kCustom, calls=%fused_computation | custom fusion | bytes 8389632 | tf_op jit(solution)/shard_map/jit(_take)/gather | solution.py:22
  21.7 0.0 copy-start.4
  21.7 13.8 %gather_fusion.1 = bf16[4096,64]{1,0:T(8,128)(2,1)S(1)} fusion(bf16[64,16384]{0,1:T(8,128)(2,1)} %bitcast.57, s32[4096]{0:T(1024)S(1)} %broadcast_clamp_fusion), kind=kCustom, calls=%fused_computation.1 | custom fusion | bytes 1064960 | tf_op jit(solution)/shard_map/jit(_take)/gather | solution.py:43
  35.5 0.0 copy-done.4
  35.5 0.0 copy-start.2
  35.5 1.5 fusion.29
  37.0 0.7 copy-done.2
  37.7 5.6 %fusion.19 = bf16[32,8,8,128]{3,2,1,0:T(8,128)(2,1)S(1)} fusion(bf16[1,32,8,128,128]{4,3,2,1,0:T(8,128)(2,1)} %param.13, bf16[64,32,8,128]{3,0,2,1:T(8,128)(2,1)S(1)} %bitcast.60, pred[32,8]{1,0:T(8,128)(4,1)S(1)} %copy.22, bf16[32,8]{1,0:T(8,128)(2,1)S(1)} %fusion.33, f32[32]{0:T(128)S(1)} %bitcast_convert_fusion), kind=kOutput, calls=%fused_computation.19 | convolution fusion | flops 541589504 | bytes 13108096 | tf_op jit(solution)/shard_map/tkrs,ftks->ftr/dot_general | solution.py:25
  43.3 0.0 copy-done.5
  43.3 2.7 %convolution_add_fusion = f32[4096,256]{1,0:T(8,128)} fusion(f32[4096,256]{1,0:T(8,128)S(1)} %fusion.29, bf16[256,64]{0,1:T(8,128)(2,1)S(1)} %copy-done.5, bf16[32,8,8,128]{3,2,1,0:T(8,128)(2,1)S(1)} %fusion.19), kind=kOutput, calls=%fused_computation.4 | convolution fusion | flops 135266304 | bytes 8945664 | tf_op jit(solution)/shard_map/dot_general | solution.py:33
  46.1 0.0 reduce-scatter.2.cloned.1.call-update
  46.1 0.0 all-gather.2.cloned.1.call-start
  46.1 54.1 %reduce-scatter.2.cloned.1.call-done = f32[512,256]{1,0:T(8,128)} async-done(((f32[4096,256]{1,0:T(8,128)}), f32[512,256]{1,0:T(8,128)}) %reduce-scatter.2.cloned.1.call-update) | async-done | bytes 524304 | tf_op jit(solution)/shard_map/reduce_scatter | solution.py:46
  100.2 0.0 copy-done
  100.2 0.0 copy-done.7
  100.2 2.0 fusion.13
  102.3 0.0 all-gather.2.cloned.1.call-update
  102.3 0.0 all-reduce.6.cloned.1.call-start
  102.4 2.1 convolution_bitcast_fusion
  104.4 26.4 %all-gather.2.cloned.1.call-done = bf16[4096,256]{1,0:T(8,128)(2,1)} async-done(((bf16[512,256]{1,0:T(8,128)(2,1)}), bf16[4096,256]{1,0:T(8,128)(2,1)}) %all-gather.2.cloned.1.call-update) | async-done | bytes 2097168 | tf_op jit(solution)/shard_map/all_gather | solution.py:62
  130.8 4.9 %fusion.30 = f32[256,64]{0,1:T(8,128)} fusion(bf16[4096,256]{1,0:T(8,128)(2,1)} %all-gather.2.cloned.1.call-done, bf16[4096,64]{1,0:T(8,128)(2,1)S(1)} %gather_fusion.1, pred[4096]{0:T(1024)(128)(4,1)S(1)} %compare_and_fusion), kind=kOutput, calls=%fused_computation.28 | convolution fusion | flops 134479872 | bytes 2691072 | tf_op jit(solution)/shard_map/dot_general | solution.py:33
  135.7 0.0 copy-done.3
  135.7 1.1 fusion.24
  136.9 0.0 all-reduce.6.cloned.1.call-update
  136.9 0.0 all-reduce.4.cloned.1.call-start
  136.9 37.4 %all-reduce.6.cloned.1.call-done = (f32[256,256]{0,1:T(8,128)}, f32[256,64]{0,1:T(8,128)}, f32[256,64]{0,1:T(8,128)}) async-done(((f32[256,256]{0,1:T(8,128)}, f32[256,64]{0,1:T(8,128)}, f32[256,64]{0,1:T(8,128)}), (f32[256,256]{0,1:T(8,128)}, f32[256,64]{0,1:T(8,128)}, f32[256,64]{0,1:T(8,128)})) %all-reduce.6.cloned.1.call-update) | async-done | bytes 393232 | tf_op jit(solution)/shard_map/psum | solution.py:9
  174.3 0.0 all-reduce.4.cloned.1.call-update
  174.3 0.0 copy-done.6
  174.3 1.0 fusion.14
  175.4 54.9 %all-reduce.4.cloned.1.call-done = f32[256,256]{0,1:T(8,128)} async-done(((f32[256,256]{0,1:T(8,128)}), f32[256,256]{0,1:T(8,128)}) %all-reduce.4.cloned.1.call-update) | async-done | bytes 262160 | tf_op jit(solution)/shard_map/psum | solution.py:10
  230.2 1.8 copy.27
  232.0 1.5 copy.43
  233.5 1.5 copy.44
  (7 shorter events, 0.0 us)
Async XLA Ops:
  7.2 93.1 %copy-start = (bf16[1,512,256]{2,1,0:T(8,128)(2,1)S(1)}, bf16[1,512,256]{2,1,0:T(8,128)(2,1)}, u32[]{:S(2)}) copy-start(bf16[1,512,256]{2,1,0:T(8,128)(2,1)} %param.17) | copy-start | bytes 786436
  7.2 9.5 %copy-start.1 = (bf16[1,64,16384]{2,1,0:T(8,128)(2,1)S(1)}, bf16[1,64,16384]{2,1,0:T(8,128)(2,1)}, u32[]{:S(2)}) copy-start(bf16[1,64,16384]{2,1,0:T(8,128)(2,1)} %param.9) | copy-start | bytes 6291460
  7.2 93.1 %reduce-scatter.2.cloned.1.call-start = ((), (), s32[]{:S(2)}) async-start(), calls=%async_computation.1 | async-start | bytes 4718592 | tf_op jit(solution)/shard_map/reduce_scatter | solution.py:46
  21.7 13.8 %copy-start.4 = (bf16[256,64]{0,1:T(8,128)(2,1)S(1)}, bf16[256,64]{0,1:T(8,128)(2,1)}, u32[]{:S(2)}) copy-start(bf16[256,64]{0,1:T(8,128)(2,1)} %param.15) | copy-start | bytes 98308
  35.5 2.2 copy-start.2
  37.7 5.7 %copy-start.5 = (bf16[256,64]{0,1:T(8,128)(2,1)S(1)}, bf16[256,64]{0,1:T(8,128)(2,1)}, u32[]{:S(2)}) copy-start(bf16[256,64]{0,1:T(8,128)(2,1)} %param.14) | copy-start | bytes 98308
  46.1 54.2 %copy-start.7 = (bf16[256,256]{1,0:T(8,128)(2,1)S(1)}, bf16[256,256]{1,0:T(8,128)(2,1)}, u32[]{:S(2)}) copy-start(bf16[256,256]{1,0:T(8,128)(2,1)} %param.16) | copy-start | bytes 393220
  46.1 84.7 %all-gather.2.cloned.1.call-start = ((), (), s32[]{:S(2)}) async-start(), calls=%async_computation.3 | async-start | bytes 2359296 | tf_op jit(solution)/shard_map/all_gather | solution.py:62
  102.3 72.0 %all-reduce.6.cloned.1.call-start = ((), (), s32[]{:S(2)}) async-start(), calls=%async_computation.4 | async-start | bytes 786432 | tf_op jit(solution)/shard_map/psum | solution.py:9
  104.4 69.9 %copy-start.6 = (f32[512,256]{1,0:T(8,128)S(1)}, f32[512,256]{1,0:T(8,128)}, u32[]{:S(2)}) copy-start(f32[512,256]{1,0:T(8,128)} %reduce-scatter.2.cloned.1.call-done) | copy-start | bytes 1572868
  130.8 4.9 %copy-start.3 = (bf16[4096,256]{1,0:T(8,128)(2,1)S(1)}, bf16[4096,256]{1,0:T(8,128)(2,1)}, u32[]{:S(2)}) copy-start(bf16[4096,256]{1,0:T(8,128)(2,1)} %all-gather.2.cloned.1.call-done) | copy-start | bytes 6291460
  136.9 93.3 %all-reduce.4.cloned.1.call-start = ((), (), s32[]{:S(2)}) async-start(), calls=%async_computation.2 | async-start | bytes 524288 | tf_op jit(solution)/shard_map/psum | solution.py:10
Sparse Core Ops, SparseCore 0:
  46.2 53.9 reduce-scatter.1
  102.9 27.8 all-gather.1
  137.0 37.2 all-reduce.5
  177.2 52.9 all-reduce.3
